TPU v7x, 256 devices: a whole 4x4x8 slice. The times are simulated.
256 devices in a mesh: replica: 16 (over x, z_hi, core), fsdp: 16 (over z_lo, y).
Axes of the slice: x: 4, y: 4, z: 8 (z_hi: 2, z_lo: 4; z = z_hi * 4 + z_lo), core: 2. Of those that a mesh axis runs over, the one named last changes fastest.
Arguments:
- activations: bfloat16 [16, 2048, 4096], P('replica', 'fsdp'), may hold values from -6 to 6
- cotangent: bfloat16 [16, 2048, 6144], P('replica', 'fsdp'), may hold values from -120 to 120
- local_weight: bfloat16 [16, 4096, 6144], P('replica', None, 'fsdp'), may hold values from -6 to 6
- outer_param: float32 [4096, 6144], P('replica', 'fsdp'), may hold values from -6 to 6
- outer_moment: float32 [4096, 6144], P('replica', 'fsdp'), may hold values from -4 to 4
Outputs:
- merged_weight: bfloat16 [16, 4096, 6144], P('replica', None, 'fsdp')
- param_new: float32 [4096, 6144], P('replica', 'fsdp')
- moment_new: float32 [4096, 6144], P('replica', 'fsdp')
All inputs are finite; a program needn't handle non-finite values.
Results may differ from a plain program's by a relative error of at most 0.01.
Values may be sent and summed in bfloat16 or wider, within the bound.
A program may use at most 128 MiB of HBM per device.

v0:
```python
import jax
import jax.numpy as jnp
from jax import lax
from jax.sharding import PartitionSpec as P


def outer_update(local_weight, outer_param, outer_moment):
    replicas = lax.axis_size("replica")
    summed = lax.psum_scatter(
        local_weight[0].astype(jnp.float32).astype(jnp.bfloat16),
        "replica",
        scatter_dimension=0,
        tiled=True,
    ).astype(jnp.float32)
    delta = outer_param - summed / replicas
    moment_new = 0.9 * outer_moment + delta
    param_new = outer_param - 0.7 * (delta + 0.9 * moment_new)
    gathered = lax.all_gather(param_new.astype(jnp.bfloat16), "replica", axis=0, tiled=True)
    return (param_new, moment_new, gathered)


def inner_step(activations, cotangent, local_weight):
    columns = lax.all_to_all(cotangent, "fsdp", split_axis=2, concat_axis=1, tiled=True)
    everyone = lax.all_gather(activations, "fsdp", axis=1, tiled=True)
    gradient = jnp.dot(everyone[0].T, columns[0], preferred_element_type=jnp.float32)
    total_square = lax.psum(jnp.sum(gradient * gradient), "fsdp")
    entries = gradient.shape[0] * gradient.shape[1] * lax.axis_size("fsdp")
    spread = jnp.sqrt(total_square / entries + 1e-06)
    return local_weight[0].astype(jnp.float32) - 0.25 * gradient / spread


def local(activations, cotangent, local_weight, outer_param, outer_moment):
    stepped = inner_step(activations, cotangent, local_weight)
    param_new, moment_new, gathered = outer_update(local_weight, outer_param, outer_moment)
    merged = (0.5 * stepped + 0.5 * gathered.astype(jnp.float32)).astype(jnp.bfloat16)
    return (merged[None], param_new, moment_new)


def solution(mesh):
    placed = (
        P("replica", "fsdp", None),
        P("replica", "fsdp", None),
        P("replica", None, "fsdp"),
        P("replica", "fsdp"),
        P("replica", "fsdp"),
    )
    return jax.shard_map(
        local,
        mesh=mesh,
        in_specs=placed,
        out_specs=(P("replica", None, "fsdp"), P("replica", "fsdp"), P("replica", "fsdp")),
        check_vma=False,
    )
```

profile of v0, /device:TPU:32, one launch (start us, length us, event | category | flops | bytes accessed | tf_op | source)
XLA Modules:
  0.0 419.4 jit_solution(11513433110572281088)
XLA Ops:
  8.0 0.0 reduce-scatter.2.cloned.1.call-start
  8.0 0.7 reduce-scatter.2.cloned.1.call-update
  8.7 0.0 all-gather.3.cloned.1.call-start
  8.8 0.5 all-gather.3.cloned.1.call-update
  9.3 0.0 all-gather.5.cloned.1.call-start
  9.4 239.7 %reduce-scatter.2.cloned.1.call-done = bf16[256,384]{1,0:T(8,128)(2,1)} async-done(((bf16[4096,384]{1,0:T(8,128)(2,1)}), bf16[256,384]{1,0:T(8,128)(2,1)}) %reduce-scatter.2.cloned.1.call-update) | async-done | bytes 196624 | tf_op jit(solution)/shard_map/reduce_scatter | solution.py:9
  249.0 2.3 fusion.3
  251.3 0.0 all-gather.5.cloned.1.call-update
  251.3 6.8 %copy.10 = bf16[1,128,6144]{1,0,2:T(2,128)(2,1)S(1)} copy(bf16[1,128,6144]{2,1,0:T(8,128)(2,1)} %param.6) | data formatting | bytes 3145728 | tf_op args[1]
  258.2 0.6 broadcast.16
  258.7 34.4 %reduce = bf16[6144,128]{1,0:T(8,128)(2,1)} reduce(bf16[6144,1,128]{2,1,0:T(2,128)(2,1)S(1)} %bitcast.16, bf16[]{:T(256)} %broadcast.16), dimensions={1}, to_apply=%bitcast.11.reduce_sub_computation | reduce | bytes 3145730
  293.1 3.6 reshape.7
  296.7 46.5 %all_to_all.15 = bf16[16,2,24576]{2,1,0:T(2,128)(2,1)} all-to-all(bf16[16,2,24576]{2,1,0:T(2,128)(2,1)S(1)} %reshape.7), channel_id=1, replica_groups=mesh['replica'=16,'fsdp'=16] {'fsdp'}, dimensions={0} | all-to-all | bytes 3145728 | tf_op jit(solution)/shard_map/all_to_all | solution.py:23
  343.2 8.1 %reshape.8 = bf16[6144,1,128]{2,1,0:T(2,128)(2,1)S(1)} reshape(bf16[16,2,24576]{2,1,0:T(2,128)(2,1)} %all_to_all.15) | data formatting | bytes 3145728
  351.3 1.3 copy.12
  352.6 2.6 copy.11
  355.3 0.0 all-gather.3.cloned.1.call-done
  355.3 0.0 copy-start
  355.3 15.7 %multiply_reduce_fusion = (f32[]{:T(128)}, f32[4096,384]{1,0:T(8,128)}) fusion(bf16[2048,384]{1,0:T(8,128)(2,1)} %bitcast.20, bf16[1,2048,4096]{2,1,0:T(8,128)(2,1)} %all-gather.3.cloned.1.call-done), kind=kOutput, calls=%fused_computation.3 | convolution fusion | flops 6445596672 | bytes 24641540 | tf_op jit(solution)/shard_map/dot_general | solution.py:25
  370.9 34.6 %psum.7 = f32[]{:T(128)} all-reduce(f32[]{:T(128)} %get-tuple-element.6), channel_id=1, replica_groups=mesh['replica'=16,'fsdp'=16] {'fsdp'}, use_global_device_ids=true, to_apply=%region_1.0 | all-reduce | flops 1 | bytes 8 | tf_op jit(solution)/shard_map/psum | solution.py:26
  406.2 0.0 all-gather.5.cloned.1.call-done
  406.2 0.0 copy-done
  406.2 5.7 %fusion.2 = bf16[1,4096,384]{2,1,0:T(8,128)(2,1)} fusion(bf16[4096,384]{1,0:T(8,128)(2,1)} %all-gather.5.cloned.1.call-done, f32[]{:T(128)S(6)} %sqrt.3, f32[4096,384]{1,0:T(8,128)} %get-tuple-element.7, bf16[1,4096,384]{2,1,0:T(8,128)(2,1)S(1)} %copy-done), kind=kLoop, calls=%fused_computation.4 | loop fusion | flops 12582912 | bytes 15728644 | tf_op jit(solution)/shard_map/broadcast_in_dim | solution.py:36
Async XLA Ops:
  8.0 241.0 %reduce-scatter.2.cloned.1.call-start = ((), (), s32[]{:S(2)}) async-start(), calls=%async_computation.3 | async-start | bytes 3342336 | tf_op jit(solution)/shard_map/reduce_scatter | solution.py:9
  8.7 346.5 %all-gather.3.cloned.1.call-start = ((), (), s32[]{:S(2)}) async-start(), calls=%async_computation.2 | async-start | bytes 17825792 | tf_op jit(solution)/shard_map/all_gather | solution.py:24
  9.3 396.9 %all-gather.5.cloned.1.call-start = ((), (), s32[]{:S(2)}) async-start(), calls=%async_computation.4 | async-start | bytes 3342336 | tf_op jit(solution)/shard_map/all_gather | solution.py:18
  355.3 51.0 %copy-start = (bf16[1,4096,384]{2,1,0:T(8,128)(2,1)S(1)}, bf16[1,4096,384]{2,1,0:T(8,128)(2,1)}, u32[]{:S(2)}) copy-start(bf16[1,4096,384]{2,1,0:T(8,128)(2,1)} %param.7) | copy-start | bytes 9437188
Sparse Core Ops, SparseCore 0:
  13.1 235.8 reduce-scatter.1
Sparse Core Ops, SparseCore 1:
  11.0 203.1 all-gather.2
  251.4 75.1 all-gather.4
where the time goes:
time: 428 us; the launch traced here: 419 us
  waiting for transfers between devices  241 us (56%)
  blocking collectives  81.1 us (19%)
  other arithmetic  42.4 us (10%)
  local copies, waits for them, and re-layouts  23 us (5%)
  between operations  16.2 us (4%)
  matrix products  15.7 us (4%)
    reduce_scatter x1, waiting for transfers between devices, outer_update(): lax.psum_scatter(local_weight[0].astype(jnp.float32).astype(jnp.bfloat16)...  240 us
    all_to_all x1, blocking collectives, inner_step(): lax.all_to_all(cotangent, 'fsdp', split_axis=2, concat_axis=1, tiled=True)  46.5 us
    psum x1, blocking collectives, inner_step(): total_square = lax.psum(jnp.sum(gradient * gradient), 'fsdp')  34.6 us
    unnamed x1, other arithmetic  34.4 us
    unnamed x7, local copies, waits for them, and re-layouts  20.4 us
    dot_general x1, matrix products, inner_step(): jnp.dot(everyone[0].T, columns[0], preferred_element_type=jnp.float32)  15.7 us
  transfers between devices with their start and end apart: 3, of which 1 were waited for; matrix products, arithmetic and copies ran while one was open for 18% of the time, Pallas kernels for 0%

commit v1 on v0

v1 whole, which is shorter than its diff:
```python
import functools

import jax
import jax.numpy as jnp
from jax import lax
from jax.experimental import pallas as pl
from jax.experimental.pallas import tpu as pltpu
from jax.sharding import PartitionSpec as P

MESH = pl.DeviceIdType.MESH
F32, BF16 = jnp.float32, jnp.bfloat16

NX, NH, NC, NZ, NY = 4, 2, 2, 4, 4
TOK, D, FF = 128, 4096, 6144
ROWS, COLS = D // NY, FF // NZ
OWN = COLS // NY
BLOCK = 256
CHUNKS = (256, 256, 256, 128, 128)
STARTS = tuple(sum(CHUNKS[:q]) for q in range(len(CHUNKS)))
Q = len(CHUNKS)


def kernel(act, cot, lw, op, om, merged, pn_out, mn_out, *scratch):
    at = scratch[:Q]
    (
        act_v, act_t, cb, gs, gr, lw_v, rsc, rss, rsx, zs, zr, part, plow, op_v, om_v, pn_v, mn_v, out_v,
        sq, sq_y, sq_z,
        loc, out_sem, a1s, a1r, a2us, a2ur, a2ds, a2dr, c1s, c1r, c2s, c2r, gss, grs,
        rcs, rcr, rxs, rxr, zhs, zhr, gzs, gzr, gxs, gxr, gcs, gcr, qys, qyr, qzs, qzr,
    ) = scratch[Q:]
    rep, fs = lax.axis_index("replica"), lax.axis_index("fsdp")
    x, zh, c = rep // 4, (rep // 2) % 2, rep % 2
    z, y = fs // 4, fs % 4

    def at_y(k):
        return (rep, z * 4 + (y + k) % 4)

    def at_z(k):
        return (rep, ((z + k) % 4) * 4 + y)

    def at_x(k):
        return (((x + k) % 4) * 4 + zh * 2 + c, fs)

    at_c = (x * 4 + zh * 2 + (1 - c), fs)
    at_h = (x * 4 + (1 - zh) * 2 + c, fs)
    up, down = (rep, lax.min(z + 1, 3) * 4 + y), (rep, lax.max(z - 1, 0) * 4 + y)

    def remote(src, dst, ss, rs, dev):
        return pltpu.make_async_remote_copy(src_ref=src, dst_ref=dst, send_sem=ss, recv_sem=rs, device_id=dev, device_id_type=MESH)

    def landed(dst, ss, rs):
        remote(dst, dst, ss, rs, at_c).wait_recv()

    barrier = pltpu.get_barrier_semaphore()
    peers = [at_y(k) for k in (1, 2, 3)] + [at_z(k) for k in (1, 2, 3)] + [at_x(k) for k in (1, 2, 3)] + [at_c, at_h]
    for dev in peers:
        pl.semaphore_signal(barrier, inc=1, device_id=dev, device_id_type=MESH)
    act_in = pltpu.make_async_copy(act, act_v, loc.at[0])
    act_in.start()
    lw_in = pltpu.make_async_copy(lw, lw_v, loc.at[1])
    lw_in.start()
    op_in = pltpu.make_async_copy(op, op_v, loc.at[2])
    op_in.start()
    om_in = pltpu.make_async_copy(om, om_v, loc.at[3])
    om_in.start()

    def cot_cols(zt):
        return cot.at[:, pl.ds(pl.multiple_of(zt * COLS, COLS), COLS)]

    def cb_slot(zt, yt):
        return cb.at[zt, pl.ds(pl.multiple_of(yt * TOK, TOK), TOK)]

    cot_in = pltpu.make_async_copy(cot_cols(z), cb_slot(z, y), loc.at[4])
    cot_in.start()
    pl.semaphore_wait(barrier, len(peers))

    sends = []

    def send(*args):
        cp = remote(*args)
        cp.start()
        sends.append(cp)

    for k in (2, 1, 3):
        send(cot_cols((z + k) % 4), cb_slot(z, y), c1s.at[k - 1], c1r.at[k - 1], at_z(k))
    send(lw.at[:, 1 - c], rsc, rcs, rcr, at_c)

    act_in.wait()

    def at_cols(q, zt, yt):
        return at[q].at[zt, :, pl.ds(pl.multiple_of(yt * TOK, TOK), TOK)]

    for q in range(Q):
        size, start = CHUNKS[q], STARTS[q]
        for k in (2, 1, 3, 0):
            col = pl.multiple_of(((y + k) % 4) * ROWS + start, 128)
            block = act_v[:, pl.ds(col, size)].T
            if k == 0:
                at[q][z, :, pl.ds(pl.multiple_of(y * TOK, TOK), TOK)] = block
            else:
                act_t[k - 1, pl.ds(start, size)] = block
                send(act_t.at[k - 1, pl.ds(start, size)], at_cols(q, z, y), a1s.at[q, k - 1], a1r.at[q, k - 1], at_y(k))

    for k in (2, 1, 3):
        send(cot_cols(z), cb_slot(z, y), c2s.at[0, k - 1], c2r.at[0, k - 1], at_y(k))

    lw_in.wait()
    landed(rsc, rcs, rcr)

    @pl.loop(0, NX * NH)
    def _(i):
        rss[i] = (lw_v[i, c].astype(F32) + rsc[i].astype(F32)).astype(BF16)

    for k in (2, 1, 3):
        send(rss.at[pl.ds(2 * ((x + k) % 4), 2)], rsx.at[pl.ds(2 * x, 2)], rxs.at[k - 1], rxr.at[k - 1], at_x(k))

    for q in range(Q):
        for k in (1, 2, 3):
            landed(at_cols(q, z, (y + 4 - k) % 4), a1s.at[q, k - 1], a1r.at[q, k - 1])

        @pl.when(z < 3)
        def _():
            remote(at[q].at[z], at[q].at[z], a2us.at[q, 0], a2ur.at[q, 0], up).start()

        @pl.when(z > 0)
        def _():
            remote(at[q].at[z], at[q].at[z], a2ds.at[q, 0], a2dr.at[q, 0], down).start()

    for k in (1, 2, 3):
        landed(rsx.at[pl.ds(2 * ((x + 4 - k) % 4), 2)], rxs.at[k - 1], rxr.at[k - 1])

    def over_x(h):
        total = rss[2 * x + h].astype(F32)
        for k in (1, 2, 3):
            total += rsx[2 * ((x + k) % 4) + h].astype(F32)
        return total

    zs[...] = over_x(1 - zh).astype(BF16)
    send(zs, zr, zhs, zhr, at_h)
    part[...] = over_x(zh)

    cot_in.wait()
    for k in (1, 3, 2):
        zt = (z + 4 - k) % 4
        landed(cb_slot(zt, y), c1s.at[k - 1], c1r.at[k - 1])
        for j in (2, 1, 3):
            send(cb_slot(zt, y), cb_slot(zt, y), c2s.at[k, j - 1], c2r.at[k, j - 1], at_y(j))

    def forward(q):
        for d in (1, 2, 3):

            @pl.when(z >= d)
            def _():
                slot = at[q].at[lax.max(z - d, 0)]
                landed(slot, a2us.at[q, d - 1], a2ur.at[q, d - 1])
                if d < 3:

                    @pl.when(z < 3)
                    def _():
                        remote(slot, slot, a2us.at[q, d], a2ur.at[q, d], up).start()

            @pl.when(z <= 3 - d)
            def _():
                slot = at[q].at[lax.min(z + d, 3)]
                landed(slot, a2ds.at[q, d - 1], a2dr.at[q, d - 1])
                if d < 3:

                    @pl.when(z > 0)
                    def _():
                        remote(slot, slot, a2ds.at[q, d], a2dr.at[q, d], down).start()

    def forwarded(q):
        for d in (0, 1, 2):

            @pl.when((z < 3) & (z >= d))
            def _():
                slot = at[q].at[lax.max(z - d, 0)]
                remote(slot, slot, a2us.at[q, d], a2ur.at[q, d], up).wait_send()

            @pl.when((z > 0) & (z <= 3 - d))
            def _():
                slot = at[q].at[lax.min(z + d, 3)]
                remote(slot, slot, a2ds.at[q, d], a2dr.at[q, d], down).wait_send()

    def plow_at(xt, ht, ct):
        return plow.at[xt * 2 + ht, ct]

    def update():
        op_in.wait()
        om_in.wait()
        landed(zr, zhs, zhr)
        outer = op_v[...]
        delta = outer - (part[...] + zr[...].astype(F32)) * (1.0 / 16.0)
        moment = 0.9 * om_v[...] + delta
        param = outer - 0.7 * (delta + 0.9 * moment)
        mn_v[...] = moment
        pn_v[...] = param
        plow[x * 2 + zh, c] = param.astype(BF16)
        mine = plow_at(x, zh, c)
        send(mine, mine, gzs, gzr, at_h)
        for k in (2, 1, 3):
            send(mine, mine, gxs.at[0, k - 1], gxr.at[0, k - 1], at_x(k))
        for v, o, s in ((pn_v, pn_out, 5), (mn_v, mn_out, 6)):
            pltpu.make_async_copy(v, o, loc.at[s]).start()

    def spread_h():
        other = plow_at(x, 1 - zh, c)
        landed(other, gzs, gzr)
        for k in (2, 1, 3):
            send(other, other, gxs.at[1, k - 1], gxr.at[1, k - 1], at_x(k))

    def spread_c():
        for h in (0, 1):
            for k in (1, 2, 3):
                landed(plow_at((x + 4 - k) % 4, zh if h == 0 else 1 - zh, c), gxs.at[h, k - 1], gxr.at[h, k - 1])
        send(plow.at[:, c], plow.at[:, c], gcs, gcr, at_c)

    def gr_rows(yt, q):
        return gr.at[pl.ds(pl.multiple_of(yt * ROWS + STARTS[q], 128), CHUNKS[q])]

    sq[...] = jnp.zeros_like(sq)

    def gradient(q):
        size = CHUNKS[q]

        @pl.loop(0, NY)
        def _(i):
            j = (y + 1 + i) % 4
            cols = pl.ds(pl.multiple_of(j * OWN, OWN), OWN)
            total = jnp.zeros((size, OWN), F32)
            for g in range(NZ):
                total += jnp.dot(at[q][g], cb[g, :, cols], preferred_element_type=F32)
            sq[...] += jnp.sum((total * total).reshape(size // 8, 8, OWN), axis=0)
            gs[i, pl.ds(STARTS[q], size)] = total.astype(BF16)

            @pl.when(i < 3)
            def _():
                remote(gs.at[i, pl.ds(STARTS[q], size)], gr_rows(y, q), gss.at[q, i], grs.at[q, i], (rep, z * 4 + j)).start()

        gr[pl.ds(pl.multiple_of(y * ROWS + STARTS[q], 128), size)] = gs[3, pl.ds(STARTS[q], size)]

    def gathered_c():
        for s in range(4):
            zt = (z + 4 - s) % 4
            for j in (1, 2, 3):
                landed(cb_slot(zt, (y + 4 - j) % 4), c2s.at[s, j - 1], c2r.at[s, j - 1])

    forward(0)
    update()
    forward(1)
    spread_h()
    forward(2)
    gathered_c()
    gradient(0)
    forward(3)
    gradient(1)
    spread_c()
    forward(4)
    gradient(2)
    gradient(3)
    gradient(4)

    for k in (1, 2, 3):
        send(sq, sq_y.at[k - 1], qys.at[k - 1], qyr.at[k - 1], at_y(k))
    for k in (1, 2, 3):
        landed(sq_y.at[k - 1], qys.at[k - 1], qyr.at[k - 1])
    sq_z[3] = sq[...] + sq_y[0] + sq_y[1] + sq_y[2]
    for k in (1, 2, 3):
        send(sq_z.at[3], sq_z.at[k - 1], qzs.at[k - 1], qzr.at[k - 1], at_z(k))
    for k in (1, 2, 3):
        landed(sq_z.at[k - 1], qzs.at[k - 1], qzr.at[k - 1])
    square = jnp.sum(sq_z[0] + sq_z[1] + sq_z[2] + sq_z[3], axis=(0, 1), keepdims=True)
    scale = 0.125 / jnp.sqrt(square * (1.0 / (D * FF)) + 1e-6)

    landed(plow.at[:, 1 - c], gcs, gcr)
    for q in range(Q):
        for i in range(3):
            landed(gr_rows((y + 3 - i) % 4, q), gss.at[q, i], grs.at[q, i])

    @pl.loop(0, D // BLOCK)
    def _(b):
        rows = pl.ds(pl.multiple_of(b * BLOCK, BLOCK), BLOCK)
        base = lw_v[b // 2, b % 2].astype(F32) + plow[b // 2, b % 2].astype(F32)
        out_v[rows] = (0.5 * base - scale * gr[rows].astype(F32)).astype(BF16)
        pltpu.make_async_copy(out_v.at[rows], merged.at[rows], out_sem).start()

    for cp in sends:
        cp.wait_send()
    for q in range(Q):
        forwarded(q)
        for i in range(3):
            j = (y + 1 + i) % 4
            remote(gs.at[i, pl.ds(STARTS[q], CHUNKS[q])], gr_rows(y, q), gss.at[q, i], grs.at[q, i], (rep, z * 4 + j)).wait_send()
    for v, o, s in ((pn_v, pn_out, 5), (mn_v, mn_out, 6)):
        pltpu.make_async_copy(v, o, loc.at[s]).wait()
    pltpu.make_async_copy(out_v, merged, out_sem).wait()


def local(activations, cotangent, local_weight, outer_param, outer_moment):
    dma = pltpu.SemaphoreType.DMA
    state = (BLOCK, OWN)
    half = (NX * NH, BLOCK, OWN)
    whole = (NX * NH, NC, BLOCK, OWN)
    scratch = [pltpu.VMEM((NZ, size, NY * TOK), BF16) for size in CHUNKS]
    scratch += [
        pltpu.VMEM((TOK, D), BF16),
        pltpu.VMEM((3, ROWS, TOK), BF16),
        pltpu.VMEM((NZ, NY * TOK, COLS), BF16),
        pltpu.VMEM((NY, ROWS, OWN), BF16),
        pltpu.VMEM((D, OWN), BF16),
        pltpu.VMEM(whole, BF16),
        pltpu.VMEM(half, BF16),
        pltpu.VMEM(half, BF16),
        pltpu.VMEM(half, BF16),
        pltpu.VMEM(state, BF16),
        pltpu.VMEM(state, BF16),
        pltpu.VMEM(state, F32),
        pltpu.VMEM(whole, BF16),
        pltpu.VMEM(state, F32),
        pltpu.VMEM(state, F32),
        pltpu.VMEM(state, F32),
        pltpu.VMEM(state, F32),
        pltpu.VMEM((D, OWN), BF16),
        pltpu.VMEM((8, OWN), F32),
        pltpu.VMEM((3, 8, OWN), F32),
        pltpu.VMEM((4, 8, OWN), F32),
    ]
    scratch += [dma((7,)), dma(())]
    scratch += [dma((Q, 3))] * 6
    scratch += [dma((3,))] * 2 + [dma((4, 3))] * 2 + [dma((Q, 3))] * 2
    scratch += [dma(())] * 2 + [dma((3,))] * 2 + [dma(())] * 4
    scratch += [dma((2, 3))] * 2 + [dma(())] * 2 + [dma((3,))] * 4
    merged, param_new, moment_new = pl.pallas_call(
        kernel,
        out_shape=(
            jax.ShapeDtypeStruct((D, OWN), BF16),
            jax.ShapeDtypeStruct(state, F32),
            jax.ShapeDtypeStruct(state, F32),
        ),
        in_specs=[pl.BlockSpec(memory_space=pl.ANY)] * 5,
        out_specs=[pl.BlockSpec(memory_space=pl.ANY)] * 3,
        scratch_shapes=scratch,
        compiler_params=pltpu.CompilerParams(collective_id=0, has_side_effects=True, vmem_limit_bytes=60 * 2**20),
        name="merge",
    )(activations[0], cotangent[0], local_weight.reshape(whole), outer_param, outer_moment)
    return (merged[None], param_new, moment_new)


def solution(mesh):
    placed = (
        P("replica", "fsdp", None),
        P("replica", "fsdp", None),
        P("replica", None, "fsdp"),
        P("replica", "fsdp"),
        P("replica", "fsdp"),
    )
    return jax.shard_map(
        local,
        mesh=mesh,
        in_specs=placed,
        out_specs=(P("replica", None, "fsdp"), P("replica", "fsdp"), P("replica", "fsdp")),
        check_vma=False,
    )
```

time: 428 us -> 169 us (0.39); the launches traced: 419 us -> 168 us
  waiting for transfers between devices: 241 us -> 0 us
  Pallas kernels: 0 us -> 162 us
  blocking collectives: 81.1 us -> 0 us
  other arithmetic: 42.4 us -> 0 us
  local copies, waits for them, and re-layouts: 23 us -> 5.44 us
  matrix products: 15.7 us -> 0 us
  between operations: 16.2 us -> 0.66 us
    reduce_scatter x1 -> x0, waiting for transfers between devices: 240 us -> none  [outer_update(): lax.psum_scatter(local_weight[0].astype(jnp.float32).astype(jnp.bfloat16)...]
    pallas_call x0 -> x1, Pallas kernels: none -> 162 us  [local(): pl.pallas_call(kernel, out_shape=(jax.ShapeDtypeStruct((D, OWN), BF16), j...]
    all_to_all x1 -> x0, blocking collectives: 46.5 us -> none  [inner_step(): lax.all_to_all(cotangent, 'fsdp', split_axis=2, concat_axis=1, tiled=True)]
    psum x1 -> x0, blocking collectives: 34.6 us -> none  [inner_step(): total_square = lax.psum(jnp.sum(gradient * gradient), 'fsdp')]
    unnamed x1 -> x0, other arithmetic: 34.4 us -> none
    dot_general x1 -> x0, matrix products: 15.7 us -> none  [inner_step(): jnp.dot(everyone[0].T, columns[0], preferred_element_type=jnp.float32)]
    unnamed x7, local copies, waits for them, and re-layouts: 20.4 us -> 5.44 us
    broadcast_in_dim x1 -> x0, other arithmetic: 5.72 us -> none  [local(): return (merged[None], param_new, moment_new)]
  transfers between devices with their start and end apart: 3 -> 0, of which waited for: 1 -> 0; matrix products, arithmetic and copies ran while one was open for 18% -> 0% of each run, Pallas kernels for 0% -> 0%
where the time goes in v1:
time: 169 us; the launch traced here: 168 us
  Pallas kernels  162 us (96%)
  local copies, waits for them, and re-layouts  5.44 us (3%)
    pallas_call x1, Pallas kernels, local(): pl.pallas_call(kernel, out_shape=(jax.ShapeDtypeStruct((D, OWN), BF16), j...  162 us
    unnamed x7, local copies, waits for them, and re-layouts  5.44 us

profile of v1, /device:TPU:32, one launch (start us, length us, event | category | flops | bytes accessed | tf_op | source)
XLA Modules:
  0.0 168.2 jit_solution(16634170965771205972)
XLA Ops:
  0.6 162.1 %merge.1 = (bf16[4096,384]{1,0:T(8,128)(2,1)}, f32[256,384]{1,0:T(8,128)}, f32[256,384]{1,0:T(8,128)}) custom-call(bf16[128,4096]{1,0:T(8,128)(2,1)} %bitcast.7, bf16[128,6144]{1,0:T(8,128)(2,1)} %bitcast.6, bf16[8,2,256,384]{3,2,1,0:T(8,128)(2,1)} %bitcast.4, f32[256,384]{1,0:T(8,128)} %op.1, f32[256,384]{1,0:T(8,128)} %om.1), custom_call_target="tpu_custom_call" | custom-call | tf_op jit(solution)/shard_map/merge/pallas_call | solution.py:333
  162.7 0.0 copy-start.1
  162.7 0.0 copy-start
  162.7 3.9 %copy.11 = bf16[1,4096,384]{2,1,0:T(8,128)(2,1)} copy(bf16[1,4096,384]{2,1,0:T(8,128)(2,1)} %bitcast.5) | data formatting | bytes 6291456
  166.7 0.0 copy-done.1
  166.7 0.7 copy.12
  167.4 0.0 copy-done
  167.4 0.7 copy.13
Async XLA Ops:
  162.7 4.0 %copy-start.1 = (f32[256,384]{1,0:T(8,128)S(1)}, f32[256,384]{1,0:T(8,128)}, u32[]{:S(2)}) copy-start(f32[256,384]{1,0:T(8,128)} %get-tuple-element.13) | copy-start | bytes 1179652
  162.7 4.7 %copy-start = (f32[256,384]{1,0:T(8,128)S(1)}, f32[256,384]{1,0:T(8,128)}, u32[]{:S(2)}) copy-start(f32[256,384]{1,0:T(8,128)} %get-tuple-element.14) | copy-start | bytes 1179652

commit v2 on v1

--- a/solution.py
+++ b/solution.py
@@ -24,9 +24,9 @@
     at = scratch[:Q]
     (
         act_v, act_t, cb, gs, gr, lw_v, rsc, rss, rsx, zs, zr, part, plow, op_v, om_v, pn_v, mn_v, out_v,
-        sq, sq_y, sq_z,
+        sq, sqs, acc,
         loc, out_sem, a1s, a1r, a2us, a2ur, a2ds, a2dr, c1s, c1r, c2s, c2r, gss, grs,
-        rcs, rcr, rxs, rxr, zhs, zhr, gzs, gzr, gxs, gxr, gcs, gcr, qys, qyr, qzs, qzr,
+        rcs, rcr, rxs, rxr, zhs, zhr, gzs, gzr, gxs, gxr, gcs, gcr, qss, qsr,
     ) = scratch[Q:]
     rep, fs = lax.axis_index("replica"), lax.axis_index("fsdp")
     x, zh, c = rep // 4, (rep // 2) % 2, rep % 2
@@ -35,8 +35,8 @@
     def at_y(k):
         return (rep, z * 4 + (y + k) % 4)
 
-    def at_z(k):
-        return (rep, ((z + k) % 4) * 4 + y)
+    def in_plane(k):
+        return (rep, ((z + k // 4) % 4) * 4 + (y + k % 4) % 4)
 
     def at_x(k):
         return (((x + k) % 4) * 4 + zh * 2 + c, fs)
@@ -52,7 +52,8 @@
         remote(dst, dst, ss, rs, at_c).wait_recv()
 
     barrier = pltpu.get_barrier_semaphore()
-    peers = [at_y(k) for k in (1, 2, 3)] + [at_z(k) for k in (1, 2, 3)] + [at_x(k) for k in (1, 2, 3)] + [at_c, at_h]
+    others = range(1, NZ * NY)
+    peers = [in_plane(k) for k in others] + [at_x(k) for k in (1, 2, 3)] + [at_c, at_h]
     for dev in peers:
         pl.semaphore_signal(barrier, inc=1, device_id=dev, device_id_type=MESH)
     act_in = pltpu.make_async_copy(act, act_v, loc.at[0])
@@ -81,16 +82,42 @@
         cp.start()
         sends.append(cp)
 
-    for k in (2, 1, 3):
-        send(cot_cols((z + k) % 4), cb_slot(z, y), c1s.at[k - 1], c1r.at[k - 1], at_z(k))
-    send(lw.at[:, 1 - c], rsc, rcs, rcr, at_c)
-
-    act_in.wait()
+    planes = (z, 1 + z % 2, (2 + 3 * z) % 5, 3 - 3 * (z // 2))
+
+    def plane_dev(i):
+        return (rep, planes[i] * 4 + y)
+
+    def c1_send(i):
+        send(cot_cols(planes[i]), cb_slot(z, y), c1s.at[i - 1], c1r.at[z], plane_dev(i))
+
+    def c1_land(i):
+        landed(cb_slot(planes[i], y), c1s.at[i - 1], c1r.at[planes[i]])
+
+    def cb_half(zt, yt, h):
+        return cb.at[zt, pl.ds(pl.multiple_of(yt * TOK + h * (TOK // 2), TOK // 2), TOK // 2)]
+
+    def c2_send(s):
+        src = cot_cols(z) if s == 0 else cb_slot(planes[s], y)
+        send(src, cb_slot(planes[s], y), c2s.at[s, 0], c2r.at[s, 0], at_y(1))
+        send(src, cb_slot(planes[s], y), c2s.at[s, 1], c2r.at[s, 1], at_y(3))
+
+    def c2_pass(s):
+        for i, k in ((0, 3), (1, 1)):
+            landed(cb_slot(planes[s], (y + k) % 4), c2s.at[s, i], c2r.at[s, i])
+            piece = cb_half(planes[s], (y + k) % 4, i)
+            send(piece, piece, c2s.at[s, 2 + i], c2r.at[s, 2 + i], at_y(4 - k))
+
+    def c2_land(s):
+        for i in (0, 1):
+            landed(cb_half(planes[s], (y + 2) % 4, i), c2s.at[s, 2 + i], c2r.at[s, 2 + i])
 
     def at_cols(q, zt, yt):
         return at[q].at[zt, :, pl.ds(pl.multiple_of(yt * TOK, TOK), TOK)]
 
-    for q in range(Q):
+    def a1_in():
+        act_in.wait()
+
+    def a1_send(q):
         size, start = CHUNKS[q], STARTS[q]
         for k in (2, 1, 3, 0):
             col = pl.multiple_of(((y + k) % 4) * ROWS + start, 128)
@@ -101,33 +128,37 @@
                 act_t[k - 1, pl.ds(start, size)] = block
                 send(act_t.at[k - 1, pl.ds(start, size)], at_cols(q, z, y), a1s.at[q, k - 1], a1r.at[q, k - 1], at_y(k))
 
-    for k in (2, 1, 3):
-        send(cot_cols(z), cb_slot(z, y), c2s.at[0, k - 1], c2r.at[0, k - 1], at_y(k))
-
-    lw_in.wait()
-    landed(rsc, rcs, rcr)
-
-    @pl.loop(0, NX * NH)
-    def _(i):
-        rss[i] = (lw_v[i, c].astype(F32) + rsc[i].astype(F32)).astype(BF16)
-
-    for k in (2, 1, 3):
-        send(rss.at[pl.ds(2 * ((x + k) % 4), 2)], rsx.at[pl.ds(2 * x, 2)], rxs.at[k - 1], rxr.at[k - 1], at_x(k))
-
-    for q in range(Q):
+    def a1_land(q):
         for k in (1, 2, 3):
             landed(at_cols(q, z, (y + 4 - k) % 4), a1s.at[q, k - 1], a1r.at[q, k - 1])
 
-        @pl.when(z < 3)
-        def _():
-            remote(at[q].at[z], at[q].at[z], a2us.at[q, 0], a2ur.at[q, 0], up).start()
-
-        @pl.when(z > 0)
-        def _():
-            remote(at[q].at[z], at[q].at[z], a2ds.at[q, 0], a2dr.at[q, 0], down).start()
-
-    for k in (1, 2, 3):
-        landed(rsx.at[pl.ds(2 * ((x + 4 - k) % 4), 2)], rxs.at[k - 1], rxr.at[k - 1])
+    def own_up(q):
+        remote(at[q].at[z], at[q].at[z], a2us.at[q, 0], a2ur.at[q, 0], up).start()
+
+    def own_down(q):
+        remote(at[q].at[z], at[q].at[z], a2ds.at[q, 0], a2dr.at[q, 0], down).start()
+
+    def own_out(q):
+        pl.when((z == 0) | (z == 2))(lambda: own_up(q))
+        pl.when((z == 1) | (z == 3))(lambda: own_down(q))
+
+    def own_in(q):
+        pl.when(z == 1)(lambda: own_up(q))
+        pl.when(z == 2)(lambda: own_down(q))
+
+    def rs_core():
+        send(lw.at[:, 1 - c], rsc, rcs, rcr, at_c)
+
+    def rs_x():
+        lw_in.wait()
+        landed(rsc, rcs, rcr)
+
+        @pl.loop(0, NX * NH)
+        def _(i):
+            rss[i] = (lw_v[i, c].astype(F32) + rsc[i].astype(F32)).astype(BF16)
+
+        for k in (2, 1, 3):
+            send(rss.at[pl.ds(2 * ((x + k) % 4), 2)], rsx.at[pl.ds(2 * x, 2)], rxs.at[k - 1], rxr.at[k - 1], at_x(k))
 
     def over_x(h):
         total = rss[2 * x + h].astype(F32)
@@ -135,39 +166,49 @@
             total += rsx[2 * ((x + k) % 4) + h].astype(F32)
         return total
 
-    zs[...] = over_x(1 - zh).astype(BF16)
-    send(zs, zr, zhs, zhr, at_h)
-    part[...] = over_x(zh)
-
-    cot_in.wait()
-    for k in (1, 3, 2):
-        zt = (z + 4 - k) % 4
-        landed(cb_slot(zt, y), c1s.at[k - 1], c1r.at[k - 1])
-        for j in (2, 1, 3):
-            send(cb_slot(zt, y), cb_slot(zt, y), c2s.at[k, j - 1], c2r.at[k, j - 1], at_y(j))
-
-    def forward(q):
-        for d in (1, 2, 3):
-
-            @pl.when(z >= d)
-            def _():
-                slot = at[q].at[lax.max(z - d, 0)]
-                landed(slot, a2us.at[q, d - 1], a2ur.at[q, d - 1])
-                if d < 3:
-
-                    @pl.when(z < 3)
-                    def _():
-                        remote(slot, slot, a2us.at[q, d], a2ur.at[q, d], up).start()
-
-            @pl.when(z <= 3 - d)
-            def _():
-                slot = at[q].at[lax.min(z + d, 3)]
-                landed(slot, a2ds.at[q, d - 1], a2dr.at[q, d - 1])
-                if d < 3:
-
-                    @pl.when(z > 0)
-                    def _():
-                        remote(slot, slot, a2ds.at[q, d], a2dr.at[q, d], down).start()
+    def rs_h():
+        for k in (1, 2, 3):
+            landed(rsx.at[pl.ds(2 * ((x + 4 - k) % 4), 2)], rxs.at[k - 1], rxr.at[k - 1])
+        zs[...] = over_x(1 - zh).astype(BF16)
+        send(zs, zr, zhs, zhr, at_h)
+        part[...] = over_x(zh)
+
+    def from_below(q, d):
+        slot = at[q].at[lax.max(z - d, 0)]
+        landed(slot, a2us.at[q, d - 1], a2ur.at[q, d - 1])
+        return slot
+
+    def from_above(q, d):
+        slot = at[q].at[lax.min(z + d, 3)]
+        landed(slot, a2ds.at[q, d - 1], a2dr.at[q, d - 1])
+        return slot
+
+    def pass_up(q, d):
+        slot = from_below(q, d)
+        remote(slot, slot, a2us.at[q, d], a2ur.at[q, d], up).start()
+
+    def pass_down(q, d):
+        slot = from_above(q, d)
+        remote(slot, slot, a2ds.at[q, d], a2dr.at[q, d], down).start()
+
+    def pass_in(q):
+        pl.when(z == 1)(lambda: pass_up(q, 1))
+        pl.when(z == 2)(lambda: pass_down(q, 1))
+
+    def pass_out(q, d):
+        pl.when(z == 2)(lambda: pass_up(q, d))
+        pl.when(z == 1)(lambda: pass_down(q, d))
+
+    def a2_land(q):
+        @pl.when(z == 3)
+        def _():
+            for d in (1, 2, 3):
+                from_below(q, d)
+
+        @pl.when(z == 0)
+        def _():
+            for d in (1, 2, 3):
+                from_above(q, d)
 
     def forwarded(q):
         for d in (0, 1, 2):
@@ -218,79 +259,77 @@
     def gr_rows(yt, q):
         return gr.at[pl.ds(pl.multiple_of(yt * ROWS + STARTS[q], 128), CHUNKS[q])]
 
-    sq[...] = jnp.zeros_like(sq)
-
     def gradient(q):
+        if q == 0:
+            cot_in.wait()
         size = CHUNKS[q]
+        rows = pl.ds(0, size)
+        for g in range(NZ):
+            term = jnp.dot(at[q][g], cb[g], preferred_element_type=F32)
+            if g == 0:
+                acc[rows] = term
+            else:
+                acc[rows] += term
 
         @pl.loop(0, NY)
         def _(i):
             j = (y + 1 + i) % 4
-            cols = pl.ds(pl.multiple_of(j * OWN, OWN), OWN)
-            total = jnp.zeros((size, OWN), F32)
-            for g in range(NZ):
-                total += jnp.dot(at[q][g], cb[g, :, cols], preferred_element_type=F32)
+            total = acc[rows, pl.ds(pl.multiple_of(j * OWN, OWN), OWN)]
             sq[...] += jnp.sum((total * total).reshape(size // 8, 8, OWN), axis=0)
             gs[i, pl.ds(STARTS[q], size)] = total.astype(BF16)
 
-            @pl.when(i < 3)
-            def _():
-                remote(gs.at[i, pl.ds(STARTS[q], size)], gr_rows(y, q), gss.at[q, i], grs.at[q, i], (rep, z * 4 + j)).start()
-
         gr[pl.ds(pl.multiple_of(y * ROWS + STARTS[q], 128), size)] = gs[3, pl.ds(STARTS[q], size)]
 
-    def gathered_c():
-        for s in range(4):
-            zt = (z + 4 - s) % 4
-            for j in (1, 2, 3):
-                landed(cb_slot(zt, (y + 4 - j) % 4), c2s.at[s, j - 1], c2r.at[s, j - 1])
-
-    forward(0)
-    update()
-    forward(1)
-    spread_h()
-    forward(2)
-    gathered_c()
-    gradient(0)
-    forward(3)
-    gradient(1)
-    spread_c()
-    forward(4)
-    gradient(2)
-    gradient(3)
-    gradient(4)
-
-    for k in (1, 2, 3):
-        send(sq, sq_y.at[k - 1], qys.at[k - 1], qyr.at[k - 1], at_y(k))
-    for k in (1, 2, 3):
-        landed(sq_y.at[k - 1], qys.at[k - 1], qyr.at[k - 1])
-    sq_z[3] = sq[...] + sq_y[0] + sq_y[1] + sq_y[2]
-    for k in (1, 2, 3):
-        send(sq_z.at[3], sq_z.at[k - 1], qzs.at[k - 1], qzr.at[k - 1], at_z(k))
-    for k in (1, 2, 3):
-        landed(sq_z.at[k - 1], qzs.at[k - 1], qzr.at[k - 1])
-    square = jnp.sum(sq_z[0] + sq_z[1] + sq_z[2] + sq_z[3], axis=(0, 1), keepdims=True)
-    scale = 0.125 / jnp.sqrt(square * (1.0 / (D * FF)) + 1e-6)
-
-    landed(plow.at[:, 1 - c], gcs, gcr)
-    for q in range(Q):
+    def g_send(q):
+        for i in (1, 0, 2):
+            send(gs.at[i, pl.ds(STARTS[q], CHUNKS[q])], gr_rows(y, q), gss.at[q, i], grs.at[q, i], at_y(i + 1))
+
+    def g_land(q):
         for i in range(3):
             landed(gr_rows((y + 3 - i) % 4, q), gss.at[q, i], grs.at[q, i])
 
-    @pl.loop(0, D // BLOCK)
-    def _(b):
-        rows = pl.ds(pl.multiple_of(b * BLOCK, BLOCK), BLOCK)
-        base = lw_v[b // 2, b % 2].astype(F32) + plow[b // 2, b % 2].astype(F32)
-        out_v[rows] = (0.5 * base - scale * gr[rows].astype(F32)).astype(BF16)
-        pltpu.make_async_copy(out_v.at[rows], merged.at[rows], out_sem).start()
+    def squares_send():
+        for i, k in enumerate(others):
+            send(sq, sqs.at[i], qss.at[i], qsr.at[i], in_plane(k))
+
+    def squares_land():
+        for i in range(len(others)):
+            landed(sqs.at[i], qss.at[i], qsr.at[i])
+
+    def finish():
+        square = sq[...]
+        for i in range(len(others)):
+            square += sqs[i]
+        square = jnp.sum(square, axis=(0, 1), keepdims=True)
+        scale = 0.125 / jnp.sqrt(square * (1.0 / (D * FF)) + 1e-6)
+
+        landed(plow.at[:, 1 - c], gcs, gcr)
+
+        @pl.loop(0, D // BLOCK)
+        def _(b):
+            rows = pl.ds(pl.multiple_of(b * BLOCK, BLOCK), BLOCK)
+            base = lw_v[b // 2, b % 2].astype(F32) + plow[b // 2, b % 2].astype(F32)
+            out_v[rows] = (0.5 * base - scale * gr[rows].astype(F32)).astype(BF16)
+            pltpu.make_async_copy(out_v.at[rows], merged.at[rows], out_sem).start()
+
+    sq[...] = jnp.zeros_like(sq)
+    steps = [
+        (c1_send, 1), (c1_send, 2), (c1_send, 3), (rs_core,), (a1_in,), (a1_send, 0), (a1_send, 1), (a1_send, 2), (a1_send, 3), (a1_send, 4),
+        (c2_send, 0), (rs_x,), (a1_land, 0), (own_out, 0), (own_in, 0), (a1_land, 1), (own_out, 1), (a1_land, 2), (own_out, 2), (a1_land, 3), (own_out, 3), (a1_land, 4), (own_out, 4),
+        (c1_land, 1), (c2_send, 1), (c2_pass, 0), (rs_h,), (c1_land, 2), (c2_send, 2), (pass_in, 0), (own_in, 1), (c1_land, 3), (c2_send, 3), (pass_in, 1), (own_in, 2),
+        (c2_pass, 1), (pass_out, 0, 1), (pass_in, 2), (own_in, 3), (pass_out, 0, 2), (update,), (c2_pass, 2), (pass_out, 1, 1), (pass_in, 3), (own_in, 4), (pass_out, 1, 2), (pass_in, 4),
+        (c2_pass, 3), (pass_out, 2, 1), (spread_h,), (pass_out, 2, 2), (pass_out, 3, 1),
+        (c2_land, 0), (c2_land, 1), (c2_land, 2), (c2_land, 3), (a2_land, 0), (gradient, 0), (g_send, 0), (pass_out, 3, 2), (pass_out, 4, 1), (a2_land, 1), (gradient, 1), (g_send, 1), (pass_out, 4, 2),
+        (spread_c,), (a2_land, 2), (gradient, 2), (g_send, 2), (a2_land, 3), (gradient, 3), (g_send, 3),
+        (a2_land, 4), (gradient, 4), (squares_send,), (g_send, 4), (squares_land,), (g_land, 0), (g_land, 1), (g_land, 2), (g_land, 3), (g_land, 4), (finish,),
+    ]
+    for step, *args in steps:
+        step(*args)
 
     for cp in sends:
         cp.wait_send()
     for q in range(Q):
         forwarded(q)
-        for i in range(3):
-            j = (y + 1 + i) % 4
-            remote(gs.at[i, pl.ds(STARTS[q], CHUNKS[q])], gr_rows(y, q), gss.at[q, i], grs.at[q, i], (rep, z * 4 + j)).wait_send()
     for v, o, s in ((pn_v, pn_out, 5), (mn_v, mn_out, 6)):
         pltpu.make_async_copy(v, o, loc.at[s]).wait()
     pltpu.make_async_copy(out_v, merged, out_sem).wait()
@@ -322,14 +361,14 @@
         pltpu.VMEM(state, F32),
         pltpu.VMEM((D, OWN), BF16),
         pltpu.VMEM((8, OWN), F32),
-        pltpu.VMEM((3, 8, OWN), F32),
-        pltpu.VMEM((4, 8, OWN), F32),
+        pltpu.VMEM((NZ * NY - 1, 8, OWN), F32),
+        pltpu.VMEM((max(CHUNKS), COLS), F32),
     ]
     scratch += [dma((7,)), dma(())]
     scratch += [dma((Q, 3))] * 6
-    scratch += [dma((3,))] * 2 + [dma((4, 3))] * 2 + [dma((Q, 3))] * 2
+    scratch += [dma((3,)), dma((4,))] + [dma((4, 4))] * 2 + [dma((Q, 3))] * 2
     scratch += [dma(())] * 2 + [dma((3,))] * 2 + [dma(())] * 4
-    scratch += [dma((2, 3))] * 2 + [dma(())] * 2 + [dma((3,))] * 4
+    scratch += [dma((2, 3))] * 2 + [dma(())] * 2 + [dma((NZ * NY - 1,))] * 2
     merged, param_new, moment_new = pl.pallas_call(
         kernel,
         out_shape=(

time: 169 us -> 147 us (0.87)
  Pallas kernels: 162 us -> 141 us
    pallas_call x1, Pallas kernels: 162 us -> 141 us  [local(): pl.pallas_call(kernel, out_shape=(jax.ShapeDtypeStruct((D, OWN), BF16), j...]
where the time goes in v2:
time: 147 us
  Pallas kernels  141 us (96%)
  local copies, waits for them, and re-layouts  5.44 us (4%)
    pallas_call x1, Pallas kernels, local(): pl.pallas_call(kernel, out_shape=(jax.ShapeDtypeStruct((D, OWN), BF16), j...  141 us
    unnamed x7, local copies, waits for them, and re-layouts  5.44 us

profile of v2, /device:TPU:32, one launch (start us, length us, event | category | flops | bytes accessed | tf_op | source)
XLA Modules:
  0.0 146.8 jit_solution(9202533634754394690)
XLA Ops:
  0.6 140.7 %merge.1 = (bf16[4096,384]{1,0:T(8,128)(2,1)}, f32[256,384]{1,0:T(8,128)}, f32[256,384]{1,0:T(8,128)}) custom-call(bf16[128,4096]{1,0:T(8,128)(2,1)} %bitcast.7, bf16[128,6144]{1,0:T(8,128)(2,1)} %bitcast.6, bf16[8,2,256,384]{3,2,1,0:T(8,128)(2,1)} %bitcast.4, f32[256,384]{1,0:T(8,128)} %op.1, f32[256,384]{1,0:T(8,128)} %om.1), custom_call_target="tpu_custom_call" | custom-call | tf_op jit(solution)/shard_map/merge/pallas_call | solution.py:372
  141.3 0.0 copy-start.1
  141.3 0.0 copy-start
  141.3 3.9 %copy.11 = bf16[1,4096,384]{2,1,0:T(8,128)(2,1)} copy(bf16[1,4096,384]{2,1,0:T(8,128)(2,1)} %bitcast.5) | data formatting | bytes 6291456
  145.3 0.0 copy-done.1
  145.3 0.7 copy.12
  146.0 0.0 copy-done
  146.0 0.7 copy.13
Async XLA Ops:
  141.3 4.0 %copy-start.1 = (f32[256,384]{1,0:T(8,128)S(1)}, f32[256,384]{1,0:T(8,128)}, u32[]{:S(2)}) copy-start(f32[256,384]{1,0:T(8,128)} %get-tuple-element.13) | copy-start | bytes 1179652
  141.3 4.7 %copy-start = (f32[256,384]{1,0:T(8,128)S(1)}, f32[256,384]{1,0:T(8,128)}, u32[]{:S(2)}) copy-start(f32[256,384]{1,0:T(8,128)} %get-tuple-element.14) | copy-start | bytes 1179652

commit v3 on v2

--- a/solution.py
+++ b/solution.py
@@ -15,17 +15,18 @@
 ROWS, COLS = D // NY, FF // NZ
 OWN = COLS // NY
 BLOCK = 256
-CHUNKS = (256, 256, 256, 128, 128)
+PIECE = 256
+CHUNKS = (128, 128, 128, 128, 128, 128, 128, 128)
 STARTS = tuple(sum(CHUNKS[:q]) for q in range(len(CHUNKS)))
 Q = len(CHUNKS)
 
 
-def kernel(act, cot, lw, op, om, merged, pn_out, mn_out, *scratch):
+def exchange(act, cot, lw, op, om, g_out, plow_out, scale_out, pn_out, mn_out, *scratch):
     at = scratch[:Q]
     (
-        act_v, act_t, cb, gs, gr, lw_v, rsc, rss, rsx, zs, zr, part, plow, op_v, om_v, pn_v, mn_v, out_v,
+        act_v, act_t, cb, gs, lw_v, rsc, rss, rsx, zs, zr, part, plow, op_v, om_v, pn_v, mn_v,
         sq, sqs, acc,
-        loc, out_sem, a1s, a1r, a2us, a2ur, a2ds, a2dr, c1s, c1r, c2s, c2r, gss, grs,
+        loc, gos, a1s, a1r, a2us, a2ur, a2ds, a2dr, c1s, c1r, c2s, c2r, gss, grs,
         rcs, rcr, rxs, rxr, zhs, zhr, gzs, gzr, gxs, gxr, gcs, gcr, qss, qsr,
     ) = scratch[Q:]
     rep, fs = lax.axis_index("replica"), lax.axis_index("fsdp")
@@ -250,14 +251,18 @@
         for k in (2, 1, 3):
             send(other, other, gxs.at[1, k - 1], gxr.at[1, k - 1], at_x(k))
 
+    def plow_own():
+        return pltpu.make_async_copy(plow.at[:, c], plow_out.at[:, c], loc.at[7])
+
     def spread_c():
         for h in (0, 1):
             for k in (1, 2, 3):
                 landed(plow_at((x + 4 - k) % 4, zh if h == 0 else 1 - zh, c), gxs.at[h, k - 1], gxr.at[h, k - 1])
-        send(plow.at[:, c], plow.at[:, c], gcs, gcr, at_c)
+        send(plow.at[:, c], plow_out.at[:, c], gcs, gcr, at_c)
+        plow_own().start()
 
     def gr_rows(yt, q):
-        return gr.at[pl.ds(pl.multiple_of(yt * ROWS + STARTS[q], 128), CHUNKS[q])]
+        return g_out.at[pl.ds(pl.multiple_of(yt * ROWS + STARTS[q], 128), CHUNKS[q])]
 
     def gradient(q):
         if q == 0:
@@ -278,13 +283,16 @@
             sq[...] += jnp.sum((total * total).reshape(size // 8, 8, OWN), axis=0)
             gs[i, pl.ds(STARTS[q], size)] = total.astype(BF16)
 
-        gr[pl.ds(pl.multiple_of(y * ROWS + STARTS[q], 128), size)] = gs[3, pl.ds(STARTS[q], size)]
+    def own_rows(q):
+        return pltpu.make_async_copy(gs.at[3, pl.ds(STARTS[q], CHUNKS[q])], gr_rows(y, q), gos.at[q])
 
     def g_send(q):
         for i in (1, 0, 2):
             send(gs.at[i, pl.ds(STARTS[q], CHUNKS[q])], gr_rows(y, q), gss.at[q, i], grs.at[q, i], at_y(i + 1))
+        own_rows(q).start()
 
     def g_land(q):
+        own_rows(q).wait()
         for i in range(3):
             landed(gr_rows((y + 3 - i) % 4, q), gss.at[q, i], grs.at[q, i])
 
@@ -301,27 +309,27 @@
         for i in range(len(others)):
             square += sqs[i]
         square = jnp.sum(square, axis=(0, 1), keepdims=True)
-        scale = 0.125 / jnp.sqrt(square * (1.0 / (D * FF)) + 1e-6)
-
-        landed(plow.at[:, 1 - c], gcs, gcr)
-
-        @pl.loop(0, D // BLOCK)
-        def _(b):
-            rows = pl.ds(pl.multiple_of(b * BLOCK, BLOCK), BLOCK)
-            base = lw_v[b // 2, b % 2].astype(F32) + plow[b // 2, b % 2].astype(F32)
-            out_v[rows] = (0.5 * base - scale * gr[rows].astype(F32)).astype(BF16)
-            pltpu.make_async_copy(out_v.at[rows], merged.at[rows], out_sem).start()
+        scale_out[...] = jnp.broadcast_to(0.125 / jnp.sqrt(square * (1.0 / (D * FF)) + 1e-6), scale_out.shape)
+        landed(plow_out.at[:, 1 - c], gcs, gcr)
+        plow_own().wait()
 
     sq[...] = jnp.zeros_like(sq)
     steps = [
-        (c1_send, 1), (c1_send, 2), (c1_send, 3), (rs_core,), (a1_in,), (a1_send, 0), (a1_send, 1), (a1_send, 2), (a1_send, 3), (a1_send, 4),
-        (c2_send, 0), (rs_x,), (a1_land, 0), (own_out, 0), (own_in, 0), (a1_land, 1), (own_out, 1), (a1_land, 2), (own_out, 2), (a1_land, 3), (own_out, 3), (a1_land, 4), (own_out, 4),
-        (c1_land, 1), (c2_send, 1), (c2_pass, 0), (rs_h,), (c1_land, 2), (c2_send, 2), (pass_in, 0), (own_in, 1), (c1_land, 3), (c2_send, 3), (pass_in, 1), (own_in, 2),
-        (c2_pass, 1), (pass_out, 0, 1), (pass_in, 2), (own_in, 3), (pass_out, 0, 2), (update,), (c2_pass, 2), (pass_out, 1, 1), (pass_in, 3), (own_in, 4), (pass_out, 1, 2), (pass_in, 4),
-        (c2_pass, 3), (pass_out, 2, 1), (spread_h,), (pass_out, 2, 2), (pass_out, 3, 1),
-        (c2_land, 0), (c2_land, 1), (c2_land, 2), (c2_land, 3), (a2_land, 0), (gradient, 0), (g_send, 0), (pass_out, 3, 2), (pass_out, 4, 1), (a2_land, 1), (gradient, 1), (g_send, 1), (pass_out, 4, 2),
-        (spread_c,), (a2_land, 2), (gradient, 2), (g_send, 2), (a2_land, 3), (gradient, 3), (g_send, 3),
-        (a2_land, 4), (gradient, 4), (squares_send,), (g_send, 4), (squares_land,), (g_land, 0), (g_land, 1), (g_land, 2), (g_land, 3), (g_land, 4), (finish,),
+        (c1_send, 1), (c1_send, 2), (c1_send, 3), (rs_core,), (a1_in,), (a1_send, 0), (a1_send, 1), (a1_send, 2),
+        (a1_send, 3), (a1_send, 4), (a1_send, 5), (a1_send, 6), (a1_send, 7), (c2_send, 0), (rs_x,), (a1_land, 0),
+        (own_out, 0), (own_in, 0), (a1_land, 1), (own_out, 1), (own_in, 1), (a1_land, 2), (own_out, 2), (a1_land, 3),
+        (own_out, 3), (a1_land, 4), (own_out, 4), (a1_land, 5), (own_out, 5), (a1_land, 6), (own_out, 6), (a1_land, 7),
+        (own_out, 7), (c1_land, 1), (c2_send, 1), (c2_pass, 0), (rs_h,), (c1_land, 2), (c2_send, 2), (pass_in, 0),
+        (own_in, 2), (c1_land, 3), (c2_send, 3), (pass_in, 1), (own_in, 3), (pass_in, 2), (own_in, 4), (pass_in, 3),
+        (own_in, 5), (c2_pass, 1), (pass_in, 4), (own_in, 6), (pass_out, 0, 1), (pass_in, 5), (own_in, 7), (pass_in, 6),
+        (pass_out, 0, 2), (pass_out, 1, 1), (pass_in, 7), (c2_pass, 2), (pass_out, 1, 2), (pass_out, 2, 1), (c2_pass, 3), (update,),
+        (pass_out, 2, 2), (pass_out, 3, 1), (c2_land, 0), (c2_land, 1), (c2_land, 2), (c2_land, 3), (pass_out, 3, 2), (pass_out, 4, 1),
+        (a2_land, 0), (gradient, 0), (g_send, 0), (a2_land, 1), (gradient, 1), (g_send, 1), (pass_out, 4, 2), (pass_out, 5, 1),
+        (a2_land, 2), (gradient, 2), (g_send, 2), (pass_out, 5, 2), (pass_out, 6, 1), (spread_h,), (a2_land, 3), (gradient, 3),
+        (g_send, 3), (pass_out, 6, 2), (pass_out, 7, 1), (a2_land, 4), (gradient, 4), (g_send, 4), (pass_out, 7, 2), (a2_land, 5),
+        (gradient, 5), (g_send, 5), (spread_c,), (a2_land, 6), (gradient, 6), (g_send, 6), (a2_land, 7), (gradient, 7),
+        (squares_send,), (g_send, 7), (squares_land,), (g_land, 0), (g_land, 1), (g_land, 2), (g_land, 3), (g_land, 4),
+        (g_land, 5), (g_land, 6), (g_land, 7), (finish,),
     ]
     for step, *args in steps:
         step(*args)
@@ -332,7 +340,23 @@
         forwarded(q)
     for v, o, s in ((pn_v, pn_out, 5), (mn_v, mn_out, 6)):
         pltpu.make_async_copy(v, o, loc.at[s]).wait()
-    pltpu.make_async_copy(out_v, merged, out_sem).wait()
+
+
+def merge(scale, g, lw, low, pn, mn, merged, pn_out, mn_out, out_v, out_sem):
+    thin = [pltpu.make_async_copy(src, dst, out_sem.at[n]) for n, (src, dst) in enumerate(((pn, pn_out), (mn, mn_out)))]
+    for cp in thin:
+        cp.start()
+
+    @pl.loop(0, D // PIECE)
+    def _(i):
+        rows = pl.ds(pl.multiple_of(i * PIECE, PIECE), PIECE)
+        base = lw[rows].astype(F32) + low[rows].astype(F32)
+        out_v[rows] = (0.5 * base - scale[0:1, 0:1] * g[rows].astype(F32)).astype(BF16)
+        pltpu.make_async_copy(out_v.at[rows], merged.at[rows], out_sem.at[2]).start()
+
+    pltpu.make_async_copy(out_v, merged, out_sem.at[2]).wait()
+    for cp in thin:
+        cp.wait()
 
 
 def local(activations, cotangent, local_weight, outer_param, outer_moment):
@@ -346,7 +370,6 @@
         pltpu.VMEM((3, ROWS, TOK), BF16),
         pltpu.VMEM((NZ, NY * TOK, COLS), BF16),
         pltpu.VMEM((NY, ROWS, OWN), BF16),
-        pltpu.VMEM((D, OWN), BF16),
         pltpu.VMEM(whole, BF16),
         pltpu.VMEM(half, BF16),
         pltpu.VMEM(half, BF16),
@@ -359,29 +382,43 @@
         pltpu.VMEM(state, F32),
         pltpu.VMEM(state, F32),
         pltpu.VMEM(state, F32),
-        pltpu.VMEM((D, OWN), BF16),
         pltpu.VMEM((8, OWN), F32),
         pltpu.VMEM((NZ * NY - 1, 8, OWN), F32),
         pltpu.VMEM((max(CHUNKS), COLS), F32),
     ]
-    scratch += [dma((7,)), dma(())]
+    scratch += [dma((8,)), dma((Q,))]
     scratch += [dma((Q, 3))] * 6
     scratch += [dma((3,)), dma((4,))] + [dma((4, 4))] * 2 + [dma((Q, 3))] * 2
     scratch += [dma(())] * 2 + [dma((3,))] * 2 + [dma(())] * 4
     scratch += [dma((2, 3))] * 2 + [dma(())] * 2 + [dma((NZ * NY - 1,))] * 2
+    grad, low, scale, param_new, moment_new = pl.pallas_call(
+        exchange,
+        out_shape=(
+            pltpu.VMEM((D, OWN), BF16),
+            pltpu.VMEM(whole, BF16),
+            pltpu.VMEM((8, 128), F32),
+            pltpu.VMEM(state, F32),
+            pltpu.VMEM(state, F32),
+        ),
+        in_specs=[pl.BlockSpec(memory_space=pl.ANY)] * 5,
+        out_specs=[pl.BlockSpec(memory_space=pl.ANY)] * 2 + [pl.BlockSpec(memory_space=pltpu.VMEM)] + [pl.BlockSpec(memory_space=pl.ANY)] * 2,
+        scratch_shapes=scratch,
+        compiler_params=pltpu.CompilerParams(collective_id=0, has_side_effects=True, vmem_limit_bytes=36 * 2**20),
+        name="exchange",
+    )(*(pltpu.with_memory_space_constraint(a, pltpu.HBM) for a in (activations[0], cotangent[0], local_weight.reshape(whole), outer_param, outer_moment)))
     merged, param_new, moment_new = pl.pallas_call(
-        kernel,
+        merge,
         out_shape=(
             jax.ShapeDtypeStruct((D, OWN), BF16),
             jax.ShapeDtypeStruct(state, F32),
             jax.ShapeDtypeStruct(state, F32),
         ),
-        in_specs=[pl.BlockSpec(memory_space=pl.ANY)] * 5,
+        in_specs=[pl.BlockSpec(memory_space=pltpu.VMEM)] * 6,
         out_specs=[pl.BlockSpec(memory_space=pl.ANY)] * 3,
-        scratch_shapes=scratch,
-        compiler_params=pltpu.CompilerParams(collective_id=0, has_side_effects=True, vmem_limit_bytes=60 * 2**20),
+        scratch_shapes=[pltpu.VMEM((D, OWN), BF16), dma((3,))],
+        compiler_params=pltpu.CompilerParams(vmem_limit_bytes=20 * 2**20),
         name="merge",
-    )(activations[0], cotangent[0], local_weight.reshape(whole), outer_param, outer_moment)
+    )(scale, grad, local_weight[0], low.reshape(D, OWN), param_new, moment_new)
     return (merged[None], param_new, moment_new)
 
 

time: 147 us -> 136 us (0.925); the launches traced: 147 us -> 134 us
  Pallas kernels: 141 us -> 133 us
  local copies, waits for them, and re-layouts: 5.44 us -> 0.01 us
    pallas_call x1 -> x2, Pallas kernels: 141 us -> 133 us  [the longest x1 130 us: local(): pl.pallas_call(exchange, out_shape=(pltpu.VMEM((D, OWN), BF16), pltpu.VME...]
    unnamed x7 -> x2, local copies, waits for them, and re-layouts: 5.44 us -> 0.01 us
where the time goes in v3:
time: 136 us; the launch traced here: 134 us
  Pallas kernels  133 us (98%)
    pallas_call x1, Pallas kernels, local(): pl.pallas_call(exchange, out_shape=(pltpu.VMEM((D, OWN), BF16), pltpu.VME...  130 us
    pallas_call x1, Pallas kernels, local(): pl.pallas_call(merge, out_shape=(jax.ShapeDtypeStruct((D, OWN), BF16), ja...  3.13 us

profile of v3, /device:TPU:32, one launch (start us, length us, event | category | flops | bytes accessed | tf_op | source)
XLA Modules:
  0.0 134.1 jit_solution(13911721899975029894)
XLA Ops:
  0.6 0.0 copy-start
  0.6 130.3 %exchange.1 = (bf16[4096,384]{1,0:T(8,128)(2,1)S(1)}, bf16[8,2,256,384]{3,2,1,0:T(8,128)(2,1)S(1)}, f32[8,128]{1,0:T(8,128)S(1)}, f32[256,384]{1,0:T(8,128)S(1)}, f32[256,384]{1,0:T(8,128)S(1)}) custom-call(bf16[128,4096]{1,0:T(8,128)(2,1)} %bitcast.10, bf16[128,6144]{1,0:T(8,128)(2,1)} %bitcast.9, bf16[8,2,256,384]{3,2,1,0:T(8,128)(2,1)} %bitcast.6, ...), custom_call_target="tpu_custom_call" | custom-call | tf_op jit(solution)/shard_map/exchange/pallas_call | solution.py:394
  130.9 0.0 copy-done
  130.9 3.1 %merge.1 = (bf16[4096,384]{1,0:T(8,128)(2,1)}, f32[256,384]{1,0:T(8,128)}, f32[256,384]{1,0:T(8,128)}) custom-call(f32[8,128]{1,0:T(8,128)S(1)} %get-tuple-element.11.scale, bf16[4096,384]{1,0:T(8,128)(2,1)S(1)} %get-tuple-element.12.g, bf16[4096,384]{1,0:T(8,128)(2,1)S(1)} %bitcast.7, bf16[4096,384]{1,0:T(8,128)(2,1)S(1)} %bitcast.8, ...), custom_call_target="tpu_custom_call" | custom-call | tf_op jit(solution)/shard_map/merge/pallas_call | solution.py:409
Async XLA Ops:
  0.6 130.3 %copy-start = (bf16[1,4096,384]{2,1,0:T(8,128)(2,1)S(1)}, bf16[1,4096,384]{2,1,0:T(8,128)(2,1)}, u32[]{:S(2)}) copy-start(bf16[1,4096,384]{2,1,0:T(8,128)(2,1)} %param.7) | copy-start | bytes 9437188

commit v4 on v3

--- a/solution.py
+++ b/solution.py
@@ -25,7 +25,7 @@
     at = scratch[:Q]
     (
         act_v, act_t, cb, gs, lw_v, rsc, rss, rsx, zs, zr, part, plow, op_v, om_v, pn_v, mn_v,
-        sq, sqs, acc,
+        sq, sqn, sqs, acc,
         loc, gos, a1s, a1r, a2us, a2ur, a2ds, a2dr, c1s, c1r, c2s, c2r, gss, grs,
         rcs, rcr, rxs, rxr, zhs, zhr, gzs, gzr, gxs, gxr, gcs, gcr, qss, qsr,
     ) = scratch[Q:]
@@ -177,19 +177,19 @@
     def from_below(q, d):
         slot = at[q].at[lax.max(z - d, 0)]
         landed(slot, a2us.at[q, d - 1], a2ur.at[q, d - 1])
-        return slot
 
     def from_above(q, d):
         slot = at[q].at[lax.min(z + d, 3)]
         landed(slot, a2ds.at[q, d - 1], a2dr.at[q, d - 1])
-        return slot
 
     def pass_up(q, d):
-        slot = from_below(q, d)
+        slot = at[q].at[lax.max(z - d, 0)]
+        from_below(q, d)
         remote(slot, slot, a2us.at[q, d], a2ur.at[q, d], up).start()
 
     def pass_down(q, d):
-        slot = from_above(q, d)
+        slot = at[q].at[lax.min(z + d, 3)]
+        from_above(q, d)
         remote(slot, slot, a2ds.at[q, d], a2dr.at[q, d], down).start()
 
     def pass_in(q):
@@ -199,17 +199,6 @@
     def pass_out(q, d):
         pl.when(z == 2)(lambda: pass_up(q, d))
         pl.when(z == 1)(lambda: pass_down(q, d))
-
-    def a2_land(q):
-        @pl.when(z == 3)
-        def _():
-            for d in (1, 2, 3):
-                from_below(q, d)
-
-        @pl.when(z == 0)
-        def _():
-            for d in (1, 2, 3):
-                from_above(q, d)
 
     def forwarded(q):
         for d in (0, 1, 2):
@@ -269,9 +258,12 @@
             cot_in.wait()
         size = CHUNKS[q]
         rows = pl.ds(0, size)
-        for g in range(NZ):
-            term = jnp.dot(at[q][g], cb[g], preferred_element_type=F32)
-            if g == 0:
+        for d in range(NZ):
+            if d > 0:
+                pl.when(z == 3)(lambda: from_below(q, d))
+                pl.when(z == 0)(lambda: from_above(q, d))
+            term = jnp.dot(at[q][planes[d]], cb[planes[d]], preferred_element_type=F32)
+            if d == 0:
                 acc[rows] = term
             else:
                 acc[rows] += term
@@ -296,16 +288,22 @@
         for i in range(3):
             landed(gr_rows((y + 3 - i) % 4, q), gss.at[q, i], grs.at[q, i])
 
+    def drain(n):
+        for cp in sends[:n]:
+            cp.wait_send()
+        del sends[:n]
+
     def squares_send():
+        sqn[...] = sq[:, 0:128] + sq[:, 128:256] + sq[:, 256:384]
         for i, k in enumerate(others):
-            send(sq, sqs.at[i], qss.at[i], qsr.at[i], in_plane(k))
+            send(sqn, sqs.at[i], qss.at[i], qsr.at[i], in_plane(k))
 
     def squares_land():
         for i in range(len(others)):
             landed(sqs.at[i], qss.at[i], qsr.at[i])
 
     def finish():
-        square = sq[...]
+        square = sqn[...]
         for i in range(len(others)):
             square += sqs[i]
         square = jnp.sum(square, axis=(0, 1), keepdims=True)
@@ -324,19 +322,19 @@
         (own_in, 5), (c2_pass, 1), (pass_in, 4), (own_in, 6), (pass_out, 0, 1), (pass_in, 5), (own_in, 7), (pass_in, 6),
         (pass_out, 0, 2), (pass_out, 1, 1), (pass_in, 7), (c2_pass, 2), (pass_out, 1, 2), (pass_out, 2, 1), (c2_pass, 3), (update,),
         (pass_out, 2, 2), (pass_out, 3, 1), (c2_land, 0), (c2_land, 1), (c2_land, 2), (c2_land, 3), (pass_out, 3, 2), (pass_out, 4, 1),
-        (a2_land, 0), (gradient, 0), (g_send, 0), (a2_land, 1), (gradient, 1), (g_send, 1), (pass_out, 4, 2), (pass_out, 5, 1),
-        (a2_land, 2), (gradient, 2), (g_send, 2), (pass_out, 5, 2), (pass_out, 6, 1), (spread_h,), (a2_land, 3), (gradient, 3),
-        (g_send, 3), (pass_out, 6, 2), (pass_out, 7, 1), (a2_land, 4), (gradient, 4), (g_send, 4), (pass_out, 7, 2), (a2_land, 5),
-        (gradient, 5), (g_send, 5), (spread_c,), (a2_land, 6), (gradient, 6), (g_send, 6), (a2_land, 7), (gradient, 7),
-        (squares_send,), (g_send, 7), (squares_land,), (g_land, 0), (g_land, 1), (g_land, 2), (g_land, 3), (g_land, 4),
-        (g_land, 5), (g_land, 6), (g_land, 7), (finish,),
+        (gradient, 0), (g_send, 0), (gradient, 1), (g_send, 1), (pass_out, 4, 2), (pass_out, 5, 1), (gradient, 2), (g_send, 2),
+        (pass_out, 5, 2), (pass_out, 6, 1), (spread_h,), (gradient, 3), (g_send, 3), (pass_out, 6, 2), (pass_out, 7, 1), (gradient, 4),
+        (g_send, 4), (pass_out, 7, 2), (gradient, 5), (g_send, 5), (spread_c,), (gradient, 6), (g_send, 6), (forwarded, 0),
+        (forwarded, 1), (forwarded, 2), (forwarded, 3), (forwarded, 4), (forwarded, 5), (drain, -6), (g_land, 0), (g_land, 1),
+        (g_land, 2), (g_land, 3), (g_land, 4), (gradient, 7), (squares_send,), (g_send, 7), (squares_land,), (g_land, 5),
+        (g_land, 6), (g_land, 7), (finish,),
     ]
     for step, *args in steps:
         step(*args)
 
     for cp in sends:
         cp.wait_send()
-    for q in range(Q):
+    for q in range(Q - 2, Q):
         forwarded(q)
     for v, o, s in ((pn_v, pn_out, 5), (mn_v, mn_out, 6)):
         pltpu.make_async_copy(v, o, loc.at[s]).wait()
@@ -383,7 +381,8 @@
         pltpu.VMEM(state, F32),
         pltpu.VMEM(state, F32),
         pltpu.VMEM((8, OWN), F32),
-        pltpu.VMEM((NZ * NY - 1, 8, OWN), F32),
+        pltpu.VMEM((8, 128), F32),
+        pltpu.VMEM((NZ * NY - 1, 8, 128), F32),
         pltpu.VMEM((max(CHUNKS), COLS), F32),
     ]
     scratch += [dma((8,)), dma((Q,))]

time: 136 us -> 134 us (0.985)
  Pallas kernels: 133 us -> 131 us
    pallas_call x1, Pallas kernels: 130 us -> 128 us  [local(): pl.pallas_call(exchange, out_shape=(pltpu.VMEM((D, OWN), BF16), pltpu.VME...]
where the time goes in v4:
time: 134 us; the launch traced here: 132 us
  Pallas kernels  131 us (98%)
    pallas_call x1, Pallas kernels, local(): pl.pallas_call(exchange, out_shape=(pltpu.VMEM((D, OWN), BF16), pltpu.VME...  128 us
    pallas_call x1, Pallas kernels, local(): pl.pallas_call(merge, out_shape=(jax.ShapeDtypeStruct((D, OWN), BF16), ja...  3.13 us

profile of v4, /device:TPU:32, one launch (start us, length us, event | category | flops | bytes accessed | tf_op | source)
XLA Modules:
  0.0 131.6 jit_solution(2812282285658780498)
XLA Ops:
  0.6 0.0 copy-start
  0.6 127.8 %exchange.1 = (bf16[4096,384]{1,0:T(8,128)(2,1)S(1)}, bf16[8,2,256,384]{3,2,1,0:T(8,128)(2,1)S(1)}, f32[8,128]{1,0:T(8,128)S(1)}, f32[256,384]{1,0:T(8,128)S(1)}, f32[256,384]{1,0:T(8,128)S(1)}) custom-call(bf16[128,4096]{1,0:T(8,128)(2,1)} %bitcast.10, bf16[128,6144]{1,0:T(8,128)(2,1)} %bitcast.9, bf16[8,2,256,384]{3,2,1,0:T(8,128)(2,1)} %bitcast.6, ...), custom_call_target="tpu_custom_call" | custom-call | tf_op jit(solution)/shard_map/exchange/pallas_call | solution.py:393
  128.4 0.0 copy-done
  128.5 3.1 %merge.1 = (bf16[4096,384]{1,0:T(8,128)(2,1)}, f32[256,384]{1,0:T(8,128)}, f32[256,384]{1,0:T(8,128)}) custom-call(f32[8,128]{1,0:T(8,128)S(1)} %get-tuple-element.11.scale, bf16[4096,384]{1,0:T(8,128)(2,1)S(1)} %get-tuple-element.12.g, bf16[4096,384]{1,0:T(8,128)(2,1)S(1)} %bitcast.7, bf16[4096,384]{1,0:T(8,128)(2,1)S(1)} %bitcast.8, ...), custom_call_target="tpu_custom_call" | custom-call | tf_op jit(solution)/shard_map/merge/pallas_call | solution.py:408
Async XLA Ops:
  0.6 127.8 %copy-start = (bf16[1,4096,384]{2,1,0:T(8,128)(2,1)S(1)}, bf16[1,4096,384]{2,1,0:T(8,128)(2,1)}, u32[]{:S(2)}) copy-start(bf16[1,4096,384]{2,1,0:T(8,128)(2,1)} %param.7) | copy-start | bytes 9437188

commit v5 on v4

--- a/solution.py
+++ b/solution.py
@@ -15,7 +15,7 @@
 ROWS, COLS = D // NY, FF // NZ
 OWN = COLS // NY
 BLOCK = 256
-PIECE = 256
+PIECE = 512
 CHUNKS = (128, 128, 128, 128, 128, 128, 128, 128)
 STARTS = tuple(sum(CHUNKS[:q]) for q in range(len(CHUNKS)))
 Q = len(CHUNKS)

time: 134 us -> 135 us (level)
  no operation moved by 1% of the time
where the time goes in v5:
time: 135 us; the launch traced here: 132 us
  Pallas kernels  131 us (97%)
    pallas_call x1, Pallas kernels, local(): pl.pallas_call(exchange, out_shape=(pltpu.VMEM((D, OWN), BF16), pltpu.VME...  128 us
    pallas_call x1, Pallas kernels, local(): pl.pallas_call(merge, out_shape=(jax.ShapeDtypeStruct((D, OWN), BF16), ja...  3.48 us

profile of v5, /device:TPU:32, one launch (start us, length us, event | category | flops | bytes accessed | tf_op | source)
XLA Modules:
  0.0 131.9 jit_solution(754315010823599574)
XLA Ops:
  0.6 0.0 copy-start
  0.6 127.8 %exchange.1 = (bf16[4096,384]{1,0:T(8,128)(2,1)S(1)}, bf16[8,2,256,384]{3,2,1,0:T(8,128)(2,1)S(1)}, f32[8,128]{1,0:T(8,128)S(1)}, f32[256,384]{1,0:T(8,128)S(1)}, f32[256,384]{1,0:T(8,128)S(1)}) custom-call(bf16[128,4096]{1,0:T(8,128)(2,1)} %bitcast.10, bf16[128,6144]{1,0:T(8,128)(2,1)} %bitcast.9, bf16[8,2,256,384]{3,2,1,0:T(8,128)(2,1)} %bitcast.6, ...), custom_call_target="tpu_custom_call" | custom-call | tf_op jit(solution)/shard_map/exchange/pallas_call | solution.py:393
  128.4 0.0 copy-done
  128.5 3.5 %merge.1 = (bf16[4096,384]{1,0:T(8,128)(2,1)}, f32[256,384]{1,0:T(8,128)}, f32[256,384]{1,0:T(8,128)}) custom-call(f32[8,128]{1,0:T(8,128)S(1)} %get-tuple-element.11.scale, bf16[4096,384]{1,0:T(8,128)(2,1)S(1)} %get-tuple-element.12.g, bf16[4096,384]{1,0:T(8,128)(2,1)S(1)} %bitcast.7, bf16[4096,384]{1,0:T(8,128)(2,1)S(1)} %bitcast.8, ...), custom_call_target="tpu_custom_call" | custom-call | tf_op jit(solution)/shard_map/merge/pallas_call | solution.py:408
Async XLA Ops:
  0.6 127.8 %copy-start = (bf16[1,4096,384]{2,1,0:T(8,128)(2,1)S(1)}, bf16[1,4096,384]{2,1,0:T(8,128)(2,1)}, u32[]{:S(2)}) copy-start(bf16[1,4096,384]{2,1,0:T(8,128)(2,1)} %param.7) | copy-start | bytes 9437188
